TPU v7x, 32 devices: a whole 2x2x4 slice. The times are simulated.
32 devices in a mesh: groups: 2 (over y), tile: 4 (over z), tm: 4 (over x, core).
Axes of the slice: x: 2, y: 2, z: 4, core: 2. Of those that a mesh axis runs over, the one named last changes fastest.
Arguments:
- shocks: bfloat16 [32768, 512], P(('groups', 'tile'), 'tm'), parts along dimension 0, may hold values from -6 to 6
- volatility: float32 [16384], P('tile'), may hold values from 0.3 to 3
Outputs:
- covariance: float32 [8, 4, 1024, 16384], P('groups', 'tm', None, 'tile'), parts along dimension 0
There are 2 independent parts, one for each index of `groups`. A program takes and returns all parts, laid end to end along the dimension named above; an argument that names none is the same for every part. Nothing has to cross between parts.
All inputs are finite; a program needn't handle non-finite values.
Results may differ from a plain program's by a relative error of at most 0.023.
Values may be sent and summed in bfloat16 or wider, within the bound.
A program may use at most 192 MiB of HBM per device.

v0:
```python
import jax
import jax.numpy as jnp
from jax import lax
from jax.sharding import PartitionSpec as P

LAGS = 64


def from_behind(value, axis, steps):
    count = lax.axis_size(axis)
    leading, last = (max(0, -steps), min(count, count - steps))
    return lax.ppermute(value, axis, [(source, source + steps) for source in range(leading, last)])


def make_band(lag_count, slab_len):
    upper = lax.broadcasted_iota(jnp.int32, (lag_count + slab_len, slab_len), 0)
    column = lax.broadcasted_iota(jnp.int32, (lag_count + slab_len, slab_len), 1)
    distance = (column + lag_count - upper).astype(jnp.float32)
    inside = (distance >= 1.0) & (distance <= lag_count)
    weights = jnp.where(inside, 1.0 - distance / (lag_count + 1.0), 0.0)
    return jnp.where(distance == 0.0, 0.5, weights)


def filter_series(series, band_matrix, first_tail):
    row_count, total_len = series.shape
    lag_count = first_tail.shape[1]
    slab_len = band_matrix.shape[1]
    slab_count = total_len // slab_len
    blocks = series.reshape(row_count, slab_count, slab_len)
    tails = jnp.concatenate(
        [first_tail[:, None, :], blocks[:, :-1, slab_len - lag_count :]], axis=1
    )
    window = jnp.concatenate([tails, blocks], axis=2)
    band_high = band_matrix.astype(jnp.bfloat16)
    band_low = (band_matrix - band_high.astype(jnp.float32)).astype(jnp.bfloat16)
    smooth = jnp.einsum("rnu,uv->rnv", window, band_high, preferred_element_type=jnp.float32)
    smooth = smooth + jnp.einsum(
        "rnu,uv->rnv", window, band_low, preferred_element_type=jnp.float32
    )
    return smooth.reshape(row_count, total_len).astype(jnp.bfloat16)


def cross_terms(left_returns, left_filtered, own_returns, own_filtered):
    dims = (((1,), (1,)), ((), ()))
    first = lax.dot_general(left_returns, own_filtered, dims, preferred_element_type=jnp.float32)
    second = lax.dot_general(left_filtered, own_returns, dims, preferred_element_type=jnp.float32)
    return first + second


def local(shocks, volatility):
    scaled = (shocks.astype(jnp.float32) * volatility[:, None]).astype(jnp.bfloat16)
    row_count, slab_len = scaled.shape
    lag_count = LAGS
    band_matrix = make_band(lag_count, slab_len)
    slab_parts = lax.axis_size("tm")
    slab_index = lax.axis_index("tm")
    tile_parts = lax.axis_size("tile")
    piece_rows = row_count // slab_parts
    tail_rows = from_behind(scaled[:, slab_len - lag_count :], "tm", 1)
    local_smooth = filter_series(scaled, band_matrix, tail_rows)
    series, smooth = (
        lax.all_gather(scaled, "tm", axis=1, tiled=True),
        lax.all_gather(local_smooth, "tm", axis=1, tiled=True),
    )
    period_count = series.shape[1]
    offset_rows = slab_index * piece_rows
    piece_returns = lax.dynamic_slice_in_dim(series, offset_rows, piece_rows, 0)
    piece_filtered = lax.dynamic_slice_in_dim(smooth, offset_rows, piece_rows, 0)
    product = cross_terms(
        lax.all_gather(piece_returns, "tile", axis=0, tiled=True),
        lax.all_gather(piece_filtered, "tile", axis=0, tiled=True),
        series,
        smooth,
    )
    result = product / period_count
    return result.reshape(tile_parts, 1, piece_rows, row_count)


def solution(mesh):
    in_specs = (P(("groups", "tile"), "tm"), P("tile"))
    out_specs = P("groups", "tm", None, "tile")
    return jax.shard_map(local, mesh=mesh, in_specs=in_specs, out_specs=out_specs, check_vma=False)
```

profile of v0, /device:TPU:0, one launch (start us, length us, event | category | flops | bytes accessed | tf_op | source)
XLA Modules:
  0.0 305.9 jit_solution(8323190046501918825)
XLA Ops:
  6.5 0.0 all-gather.5.cloned.1.call-start
  6.5 1.5 copy.4
  8.0 1.9 multiply_convert_fusion
  9.9 0.0 all-gather.5.cloned.1.call-update
  10.0 0.0 all-gather.9.cloned.1.call-start
  10.0 1.1 slice.4
  11.1 2.4 collective-permute-start
  13.5 0.2 fusion.29
  13.7 1.3 collective-permute-done
  15.0 0.8 fusion.1
  15.8 1.9 fusion
  17.6 0.0 all-gather.9.cloned.1.call-update
  17.6 0.0 all-gather.7.cloned.1.call-start
  17.7 29.6 %all-gather.5.cloned.1.call-done = bf16[4096,512]{0,1:T(8,128)(2,1)} async-done(((bf16[4096,128]{0,1:T(8,128)(2,1)}), bf16[4096,512]{0,1:T(8,128)(2,1)}) %all-gather.5.cloned.1.call-update) | async-done | bytes 4194320 | tf_op jit(solution)/shard_map/all_gather | solution.py:62
  47.3 2.3 constant_dynamic-slice_fusion.1
  49.6 0.0 all-gather.7.cloned.1.call-update
  49.6 0.0 all-gather.11.cloned.1.call-start
  49.6 35.4 %all-gather.9.cloned.1.call-done = bf16[4096,512]{1,0:T(8,128)(2,1)} async-done(((bf16[4096,128]{1,0:T(8,128)(2,1)}), bf16[4096,512]{1,0:T(8,128)(2,1)}) %all-gather.9.cloned.1.call-update) | async-done | bytes 4194320 | tf_op jit(solution)/shard_map/all_gather | solution.py:63
  85.0 2.3 constant_dynamic-slice_fusion
  87.2 0.0 all-gather.11.cloned.1.call-update
  87.3 80.1 %all-gather.7.cloned.1.call-done = bf16[4096,512]{0,1:T(8,128)(2,1)} async-done(((bf16[1024,512]{0,1:T(8,128)(2,1)}), bf16[4096,512]{0,1:T(8,128)(2,1)}) %all-gather.7.cloned.1.call-update) | async-done | bytes 4194320 | tf_op jit(solution)/shard_map/all_gather | solution.py:70
  167.4 30.9 %fusion.24 = f32[4096,4096]{1,0:T(8,128)} fusion(bf16[4096,512]{0,1:T(8,128)(2,1)} %all-gather.7.cloned.1.call-done, bf16[4096,512]{1,0:T(8,128)(2,1)} %all-gather.9.cloned.1.call-done), kind=kOutput, calls=%fused_computation.34 | convolution fusion | flops 17179869184 | bytes 75497472 | tf_op jit(solution)/shard_map/dot_general | solution.py:45
  198.3 49.8 %all-gather.11.cloned.1.call-done = bf16[4096,512]{1,0:T(8,128)(2,1)} async-done(((bf16[1024,512]{1,0:T(8,128)(2,1)}), bf16[4096,512]{1,0:T(8,128)(2,1)}) %all-gather.11.cloned.1.call-update) | async-done | bytes 4194320 | tf_op jit(solution)/shard_map/all_gather | solution.py:71
  248.1 51.2 %add_multiply_fusion = f32[4096,4096]{1,0:T(8,128)} fusion(f32[4096,4096]{1,0:T(8,128)} %fusion.24, bf16[4096,512]{1,0:T(8,128)(2,1)} %all-gather.11.cloned.1.call-done, bf16[4096,512]{0,1:T(8,128)(2,1)} %all-gather.5.cloned.1.call-done), kind=kOutput, calls=%fused_computation | convolution fusion | flops 17213423616 | bytes 142606336 | tf_op jit(solution)/shard_map/dot_general | solution.py:46
  (3 shorter events, 0.0 us)
Async XLA Ops:
  6.5 7.0 %copy-start = (f32[4096]{0:T(1024)S(1)}, f32[4096]{0:T(1024)}, u32[]{:S(2)}) copy-start(f32[4096]{0:T(1024)} %param.3) | copy-start | bytes 49156
  6.5 40.8 %all-gather.5.cloned.1.call-start = ((), (), s32[]{:S(2)}) async-start(), calls=%async_computation | async-start | bytes 5242880 | tf_op jit(solution)/shard_map/all_gather | solution.py:62
  10.0 75.0 %all-gather.9.cloned.1.call-start = ((), (), s32[]{:S(2)}) async-start(), calls=%async_computation.2 | async-start | bytes 5242880 | tf_op jit(solution)/shard_map/all_gather | solution.py:63
  11.1 3.9 %collective-permute-start = (bf16[4096,64]{0,1:T(8,128)(2,1)S(1)}, bf16[4096,64]{0,1:T(8,128)(2,1)S(1)}, u32[]{:S(2)}, u32[]{:S(2)}) collective-permute-start(bf16[4096,64]{0,1:T(8,128)(2,1)S(1)} %slice.4), channel_id=1, source_target_pairs={{0,1},{1,2},{2,3},{4,5},{5,6},{6,7},{8,9},{9,10},{10,11},{12,13},{... | collective-permute-start | bytes 1572872 | tf_op jit(solution)/shard_map/ppermute | solution.py:12
  17.6 149.7 %all-gather.7.cloned.1.call-start = ((), (), s32[]{:S(2)}) async-start(), calls=%async_computation.1 | async-start | bytes 5242880 | tf_op jit(solution)/shard_map/all_gather | solution.py:70
  49.6 198.5 %all-gather.11.cloned.1.call-start = ((), (), s32[]{:S(2)}) async-start(), calls=%async_computation.3 | async-start | bytes 5242880 | tf_op jit(solution)/shard_map/all_gather | solution.py:71
Sparse Core Ops, SparseCore 0:
  10.1 37.1 all-gather.4
  48.8 36.0 all-gather.8
  86.6 80.7 all-gather.6
  168.8 79.2 all-gather.10
where the time goes:
time: 306 us
  waiting for transfers between devices  196 us (64%)
  matrix products  84.8 us (28%)
  between operations  13.2 us (4%)
  local copies, waits for them, and re-layouts  7.1 us (2%)
    all_gather x1, waiting for transfers between devices, local(): lax.all_gather(piece_returns, 'tile', axis=0, tiled=True)  80.1 us
    dot_general x1, matrix products, cross_terms(): lax.dot_general(left_filtered, own_returns, dims, preferred_element_type=...  51.2 us
    all_gather x1, waiting for transfers between devices, local(): lax.all_gather(piece_filtered, 'tile', axis=0, tiled=True)  49.8 us
    all_gather x1, waiting for transfers between devices, local(): lax.all_gather(local_smooth, 'tm', axis=1, tiled=True)  35.4 us
    dot_general x1, matrix products, cross_terms(): lax.dot_general(left_returns, own_filtered, dims, preferred_element_type=...  30.9 us
    all_gather x1, waiting for transfers between devices, local(): lax.all_gather(scaled, 'tm', axis=1, tiled=True)  29.6 us
  transfers between devices with their start and end apart: 5, of which 5 were waited for; matrix products, arithmetic and copies ran while one was open for 13% of the time, Pallas kernels for 0%

commit v1 on v0

v1 whole, which is shorter than its diff:
```python
import jax
import jax.numpy as jnp
from jax import lax
from jax.experimental import pallas as pl
from jax.experimental.pallas import tpu as pltpu
from jax.sharding import PartitionSpec as P

LAGS = 64


def swap(value, axis, mask):
    count = lax.axis_size(axis)
    return lax.ppermute(value, axis, [(source, source ^ mask) for source in range(count)])


def pass_on(value, axis):
    count = lax.axis_size(axis)
    return lax.ppermute(value, axis, [(source, (source + 1) % count) for source in range(count)])


def block_kernel(part_count, block_ref, *refs):
    parts, weighted_ref, out_ref = refs[:part_count], refs[part_count], refs[-1]
    rows = jnp.concatenate([part[...] for part in parts], axis=1)
    out_ref[0, 0] = jnp.dot(rows, weighted_ref[...], preferred_element_type=jnp.float32)


def write_block(block, parts, weighted, whole, block_count):
    piece_rows, slab_len = parts[0].shape
    period_count, column_count = weighted.shape
    row_step = min(piece_rows, 256)
    column_step = min(column_count, 2048)
    part_spec = pl.BlockSpec((row_step, slab_len), lambda c, r, b: (r, 0))
    in_specs = [part_spec] * len(parts)
    in_specs.append(pl.BlockSpec((period_count, column_step), lambda c, r, b: (0, c)))
    operands = [block, *parts, weighted]
    aliases = {}
    if whole is not None:
        in_specs.append(pl.BlockSpec(memory_space=pl.ANY))
        aliases = {len(operands): 0}
        operands.append(whole)
    return pl.pallas_call(
        lambda *refs: block_kernel(len(parts), *refs),
        out_shape=jax.ShapeDtypeStruct((block_count, 1, piece_rows, column_count), jnp.float32),
        grid_spec=pltpu.PrefetchScalarGridSpec(
            num_scalar_prefetch=1,
            grid=(column_count // column_step, piece_rows // row_step),
            in_specs=in_specs,
            out_specs=pl.BlockSpec(
                (1, 1, row_step, column_step), lambda c, r, b: (b[0], 0, r, c)
            ),
        ),
        input_output_aliases=aliases,
        compiler_params=pltpu.CompilerParams(vmem_limit_bytes=32 * 2**20),
        cost_estimate=pl.CostEstimate(
            flops=2 * piece_rows * period_count * column_count,
            bytes_accessed=4 * piece_rows * column_count + 2 * period_count * column_count,
            transcendentals=0,
        ),
    )(*operands)


def local(shocks, volatility):
    scaled = (shocks.astype(jnp.float32) * volatility[:, None]).astype(jnp.bfloat16)
    row_count, slab_len = scaled.shape
    slab_parts = lax.axis_size("tm")
    tile_parts = lax.axis_size("tile")
    slab_index = lax.axis_index("tm")
    tile_index = lax.axis_index("tile")
    piece_rows = row_count // slab_parts
    period_count = slab_parts * slab_len

    parts = []
    for mask in range(slab_parts):
        other = (slab_index ^ mask) * piece_rows
        rows = lax.dynamic_slice_in_dim(scaled, other, piece_rows, 0)
        parts.append(swap(rows, "tm", mask) if mask else rows)

    arrived = [parts]
    for _ in range(tile_parts - 1):
        arrived.append([pass_on(part, "tile") for part in arrived[-1]])

    pieces = jnp.stack(parts)[None]
    mask = slab_parts // 2
    masks = [0]
    while mask:
        pieces = jnp.concatenate([pieces, swap(pieces, "tm", mask)], axis=0)
        masks = masks + [m ^ mask for m in masks]
        mask //= 2
    ordered = jnp.stack([
        jnp.concatenate([pieces[at, m ^ q] for m in range(slab_parts)], axis=1)
        for at, q in sorted(enumerate(masks), key=lambda pair: pair[1])
    ])
    series = jnp.concatenate(
        [
            lax.dynamic_index_in_dim(ordered, slab_index ^ p, 0, keepdims=False)
            for p in range(slab_parts)
        ],
        axis=0,
    )

    place = jnp.arange(period_count, dtype=jnp.int32)
    time = ((place // slab_len) ^ slab_index) * slab_len + place % slab_len
    band = jnp.maximum(0, LAGS + 1 - jnp.abs(time[:, None] - time[None, :])).astype(jnp.bfloat16)
    weighted = lax.dot_general(
        band, series, (((1,), (1,)), ((), ())), preferred_element_type=jnp.float32
    )
    weighted = (weighted * (1.0 / ((LAGS + 1) * period_count))).astype(jnp.bfloat16)

    whole = None
    for step in range(tile_parts):
        block = lax.rem(tile_index - step + tile_parts, tile_parts).reshape(1)
        whole = write_block(block, arrived[step], weighted, whole, tile_parts)
    return whole


def solution(mesh):
    in_specs = (P(("groups", "tile"), "tm"), P("tile"))
    out_specs = P("groups", "tm", None, "tile")
    return jax.shard_map(local, mesh=mesh, in_specs=in_specs, out_specs=out_specs, check_vma=False)
```

time: 306 us -> 147 us (0.48)
  waiting for transfers between devices: 196 us -> 79.6 us
  matrix products: 84.8 us -> 9.22 us
  Pallas kernels: 0 us -> 36.7 us
  between operations: 13.2 us -> 0.17 us
  starting transfers between devices: 2.52 us -> 13 us
  local copies, waits for them, and re-layouts: 7.1 us -> 3.44 us
    all_gather x4 -> x0, waiting for transfers between devices: 195 us -> none  [the longest x1 80.1 us: local(): lax.all_gather(piece_returns, 'tile', axis=0, tiled=True)]
    ppermute x1 -> x17, waiting for transfers between devices: 1.26 us -> 79.6 us  [the longest x12 43.8 us: pass_on(): lax.ppermute(value, axis, [(source, (source + 1) % count) for source in r...]
    dot_general x4 -> x1, matrix products: 84.8 us -> 9.22 us  [local(): lax.dot_general(band, series, (((1,), (1,)), ((), ())), preferred_element...]
    pallas_call x0 -> x4, Pallas kernels: none -> 36.7 us  [write_block(): pl.pallas_call(lambda *refs: block_kernel(len(parts), *refs), out_shape=j...]
    ppermute x1 -> x17, starting transfers between devices: 2.39 us -> 13 us  [the longest x12 8.22 us: pass_on(): lax.ppermute(value, axis, [(source, (source + 1) % count) for source in r...]
    dynamic_slice x2 -> x1, local copies, waits for them, and re-layouts: 4.53 us -> 0.08 us  [local(): rows = lax.dynamic_slice_in_dim(scaled, other, piece_rows, 0)]
    squeeze x0 -> x4, local copies, waits for them, and re-layouts: none -> 3.35 us  [the longest x3 3.07 us: local(): pieces[at, m ^ q]]
  transfers between devices with their start and end apart: 5 -> 17, of which waited for: 5 -> 9; matrix products, arithmetic and copies ran while one was open for 13% -> 9% of each run, Pallas kernels for 0% -> 19%
where the time goes in v1:
time: 147 us
  waiting for transfers between devices  79.6 us (54%)
  Pallas kernels  36.7 us (25%)
  starting transfers between devices  13 us (9%)
  matrix products  9.22 us (6%)
  other arithmetic  4.58 us (3%)
  local copies, waits for them, and re-layouts  3.44 us (2%)
    ppermute x12, waiting for transfers between devices, pass_on(): lax.ppermute(value, axis, [(source, (source + 1) % count) for source in r...  43.8 us
    pallas_call x4, Pallas kernels, write_block(): pl.pallas_call(lambda *refs: block_kernel(len(parts), *refs), out_shape=j...  36.7 us
    ppermute x5, waiting for transfers between devices, swap(): lax.ppermute(value, axis, [(source, source ^ mask) for source in range(co...  35.8 us
    dot_general x1, matrix products, local(): lax.dot_general(band, series, (((1,), (1,)), ((), ())), preferred_element...  9.22 us
    ppermute x12, starting transfers between devices, pass_on(): lax.ppermute(value, axis, [(source, (source + 1) % count) for source in r...  8.22 us
    ppermute x5, starting transfers between devices, swap(): lax.ppermute(value, axis, [(source, source ^ mask) for source in range(co...  4.79 us
    squeeze x3, local copies, waits for them, and re-layouts, local(): pieces[at, m ^ q]  3.07 us
  transfers between devices with their start and end apart: 17, of which 9 were waited for; matrix products, arithmetic and copies ran while one was open for 9% of the time, Pallas kernels for 19%

profile of v1, /device:TPU:0, one launch (start us, length us, event | category | flops | bytes accessed | tf_op | source)
XLA Modules:
  0.0 146.7 jit_solution(5528055568161953505)
XLA Ops:
  0.0 1.8 %multiply_convert_fusion.1 = bf16[4096,128]{1,0:T(8,128)(2,1)S(1)} fusion(bf16[4096,128]{1,0:T(8,128)(2,1)} %param.2, f32[4096]{0:T(1024)} %param.3), kind=kLoop, calls=%fused_computation.10 | loop fusion | flops 1572864 | bytes 2113536 | tf_op jit(solution)/shard_map/convert_element_type | solution.py:63
  2.4 2.6 %collective-permute-start.7 = (bf16[1024,128]{1,0:T(8,128)(2,1)S(1)}, bf16[1024,128]{1,0:T(8,128)(2,1)S(1)}, u32[]{:S(2)}, u32[]{:S(2)}) collective-permute-start(bf16[1024,128]{1,0:T(8,128)(2,1)S(1)} %get-tuple-element.26), channel_id=1, source_target_pairs={{0,2},{1,3},{2,0},{3,1},{4,6},{5,7},{6,4},{7,5},{8,10},{9,11},{10,... | collective-permute-start | bytes 786440 | tf_op jit(solution)/shard_map/ppermute | solution.py:13
  5.0 7.1 %collective-permute-done.7.refs_3_ = bf16[1024,128]{1,0:T(8,128)(2,1)S(1)} collective-permute-done((bf16[1024,128]{1,0:T(8,128)(2,1)S(1)}, bf16[1024,128]{1,0:T(8,128)(2,1)S(1)}, u32[]{:S(2)}, u32[]{:S(2)}) %collective-permute-start.7) | collective-permute-done | bytes 262176 | tf_op jit(solution)/shard_map/ppermute | solution.py:13
  12.1 5.1 %collective-permute-done.11.refs_4_ = bf16[1024,128]{1,0:T(8,128)(2,1)S(1)} collective-permute-done((bf16[1024,128]{1,0:T(8,128)(2,1)S(1)}, bf16[1024,128]{1,0:T(8,128)(2,1)S(1)}, u32[]{:S(2)}, u32[]{:S(2)}) %collective-permute-start.11) | collective-permute-done | bytes 262176 | tf_op jit(solution)/shard_map/ppermute | solution.py:13
  17.3 1.6 %collective-permute-start.15 = (bf16[1,4,1024,128]{3,2,1,0:T(8,128)(2,1)S(1)}, bf16[1,4,1024,128]{3,2,1,0:T(8,128)(2,1)S(1)}, u32[]{:S(2)}, u32[]{:S(2)}) collective-permute-start(bf16[1,4,1024,128]{3,2,1,0:T(8,128)(2,1)S(1)} %maximum_bitcast_fusion), channel_id=1, source_target_pairs={{0,2},{1,3},{2,0},{3,1},{4,6},{5,7},{6,4},{7,5},{8,10},{9,11},{10,... | collective-permute-start | bytes 3145736 | tf_op jit(solution)/shard_map/ppermute | solution.py:13
  19.0 23.6 %collective-permute-done.15 = bf16[1,4,1024,128]{3,2,1,0:T(8,128)(2,1)S(1)} collective-permute-done((bf16[1,4,1024,128]{3,2,1,0:T(8,128)(2,1)S(1)}, bf16[1,4,1024,128]{3,2,1,0:T(8,128)(2,1)S(1)}, u32[]{:S(2)}, u32[]{:S(2)}) %collective-permute-start.15) | collective-permute-done | bytes 1048608 | tf_op jit(solution)/shard_map/ppermute | solution.py:13
  42.6 1.6 %pad_maximum_fusion.1 = bf16[2,4,1024,128]{3,2,1,0:T(8,128)(2,1)} fusion(bf16[1,4,1024,128]{3,2,1,0:T(8,128)(2,1)S(1)} %collective-permute-done.15, bf16[1,4,1024,128]{3,2,1,0:T(8,128)(2,1)S(1)} %maximum_bitcast_fusion), kind=kLoop, calls=%fused_computation.9 | loop fusion | flops 1048576 | bytes 4194304 | tf_op jit(solution)/shard_map/concatenate | solution.py:86
  44.2 1.9 %collective-permute-start = (bf16[1024,128]{1,0:T(8,128)(2,1)S(1)}, bf16[1024,128]{1,0:T(8,128)(2,1)S(1)}, u32[]{:S(2)}, u32[]{:S(2)}) collective-permute-start(bf16[1024,128]{1,0:T(8,128)(2,1)S(1)} %get-tuple-element.28.refs_1_), channel_id=1, source_target_pairs={{0,4},{4,8},{8,12},{12,0},{1,5},{5,9},{9,13},{13,1},{2,6},{6,10},{... | collective-permute-start | bytes 786440 | tf_op jit(solution)/shard_map/ppermute | solution.py:18
  46.1 1.6 %collective-permute-start.12 = (bf16[1024,128]{1,0:T(8,128)(2,1)S(1)}, bf16[1024,128]{1,0:T(8,128)(2,1)S(1)}, u32[]{:S(2)}, u32[]{:S(2)}) collective-permute-start(bf16[1024,128]{1,0:T(8,128)(2,1)S(1)} %collective-permute-done.11.refs_4_), channel_id=1, source_target_pairs={{0,4},{4,8},{8,12},{12,0},{1,5},{5,9},{9,13},{13,1},{2,6},{6,10},{... | collective-permute-start | bytes 786440 | tf_op jit(solution)/shard_map/ppermute | solution.py:18
  47.7 1.6 %collective-permute-start.4 = (bf16[1024,128]{1,0:T(8,128)(2,1)S(1)}, bf16[1024,128]{1,0:T(8,128)(2,1)S(1)}, u32[]{:S(2)}, u32[]{:S(2)}) collective-permute-start(bf16[1024,128]{1,0:T(8,128)(2,1)S(1)} %collective-permute-done.3.refs_2_), channel_id=1, source_target_pairs={{0,4},{4,8},{8,12},{12,0},{1,5},{5,9},{9,13},{13,1},{2,6},{6,10},{... | collective-permute-start | bytes 786440 | tf_op jit(solution)/shard_map/ppermute | solution.py:18
  49.4 5.9 %collective-permute-done.refs_1_ = bf16[1024,128]{1,0:T(8,128)(2,1)S(1)} collective-permute-done((bf16[1024,128]{1,0:T(8,128)(2,1)S(1)}, bf16[1024,128]{1,0:T(8,128)(2,1)S(1)}, u32[]{:S(2)}, u32[]{:S(2)}) %collective-permute-start) | collective-permute-done | bytes 262176 | tf_op jit(solution)/shard_map/ppermute | solution.py:18
  55.3 5.6 %collective-permute-done.12.refs_4_ = bf16[1024,128]{1,0:T(8,128)(2,1)S(1)} collective-permute-done((bf16[1024,128]{1,0:T(8,128)(2,1)S(1)}, bf16[1024,128]{1,0:T(8,128)(2,1)S(1)}, u32[]{:S(2)}, u32[]{:S(2)}) %collective-permute-start.12) | collective-permute-done | bytes 262176 | tf_op jit(solution)/shard_map/ppermute | solution.py:18
  60.9 5.6 %collective-permute-done.4.refs_2_ = bf16[1024,128]{1,0:T(8,128)(2,1)S(1)} collective-permute-done((bf16[1024,128]{1,0:T(8,128)(2,1)S(1)}, bf16[1024,128]{1,0:T(8,128)(2,1)S(1)}, u32[]{:S(2)}, u32[]{:S(2)}) %collective-permute-start.4) | collective-permute-done | bytes 262176 | tf_op jit(solution)/shard_map/ppermute | solution.py:18
  66.5 5.6 %collective-permute-done.8.refs_3_ = bf16[1024,128]{1,0:T(8,128)(2,1)S(1)} collective-permute-done((bf16[1024,128]{1,0:T(8,128)(2,1)S(1)}, bf16[1024,128]{1,0:T(8,128)(2,1)S(1)}, u32[]{:S(2)}, u32[]{:S(2)}) %collective-permute-start.8) | collective-permute-done | bytes 262176 | tf_op jit(solution)/shard_map/ppermute | solution.py:18
  73.5 4.2 %collective-permute-done.1.refs_1_ = bf16[1024,128]{1,0:T(8,128)(2,1)S(1)} collective-permute-done((bf16[1024,128]{1,0:T(8,128)(2,1)S(1)}, bf16[1024,128]{1,0:T(8,128)(2,1)S(1)}, u32[]{:S(2)}, u32[]{:S(2)}) %collective-permute-start.1) | collective-permute-done | bytes 262176 | tf_op jit(solution)/shard_map/ppermute | solution.py:18
  77.8 16.8 %collective-permute-done.9.refs_3_ = bf16[1024,128]{1,0:T(8,128)(2,1)S(1)} collective-permute-done((bf16[1024,128]{1,0:T(8,128)(2,1)S(1)}, bf16[1024,128]{1,0:T(8,128)(2,1)S(1)}, u32[]{:S(2)}, u32[]{:S(2)}) %collective-permute-start.9) | collective-permute-done | bytes 262176 | tf_op jit(solution)/shard_map/ppermute | solution.py:18
  94.6 1.5 %collective-permute-start.14 = (bf16[1024,128]{1,0:T(8,128)(2,1)S(1)}, bf16[1024,128]{1,0:T(8,128)(2,1)S(1)}, u32[]{:S(2)}, u32[]{:S(2)}) collective-permute-start(bf16[1024,128]{1,0:T(8,128)(2,1)S(1)} %collective-permute-done.13.refs_4_), channel_id=1, source_target_pairs={{0,4},{4,8},{8,12},{12,0},{1,5},{5,9},{9,13},{13,1},{2,6},{6,10},{... | collective-permute-start | bytes 786440 | tf_op jit(solution)/shard_map/ppermute | solution.py:18
  96.1 1.6 %collective-permute-start.6 = (bf16[1024,128]{1,0:T(8,128)(2,1)S(1)}, bf16[1024,128]{1,0:T(8,128)(2,1)S(1)}, u32[]{:S(2)}, u32[]{:S(2)}) collective-permute-start(bf16[1024,128]{1,0:T(8,128)(2,1)S(1)} %collective-permute-done.5.refs_2_), channel_id=1, source_target_pairs={{0,4},{4,8},{8,12},{12,0},{1,5},{5,9},{9,13},{13,1},{2,6},{6,10},{... | collective-permute-start | bytes 786440 | tf_op jit(solution)/shard_map/ppermute | solution.py:18
  98.0 1.7 %slice_bitcast_fusion.11 = (bf16[1024,128]{1,0:T(8,128)(2,1)S(1)}, bf16[1024,128]{1,0:T(8,128)(2,1)S(1)}, bf16[1024,128]{1,0:T(8,128)(2,1)S(1)}, bf16[1024,128]{...) fusion(bf16[2,4,1024,128]{3,2,1,0:T(8,128)(2,1)} %collective-pe, ...), kind=kLoop, calls=%fused_computation.36 | loop fusion | bytes 4194304 | tf_op jit(solution)/shard_map/squeeze | solution.py:90
  100.8 9.2 %multiply_convert_fusion.refs_5_ = bf16[512,4096]{1,0:T(8,128)(2,1)S(1)} fusion(bf16[1024,512]{1,0:T(8,128)(2,1)S(1)} %get-tuple-element.6, bf16[1024,512]{1,0:T(8,128)(2,1)S(1)} %get-tuple-element.7, bf16[1024,512]{1,0:T(8,128)(2,1)S(1)} %get-tuple-element.8, bf16[1024,512]{1,0:T(8,128)(2,1)S(1)} %get-tuple-element.5, s32[512]{0:T(512)S(1)} %fusion.17), kind=kOutput, calls=%fused_computation | convolution fusion | flops 2169765888 | bytes 8390656 | tf_op jit(solution)/shard_map/dot_general | solution.py:104
  110.0 9.2 %shard_map.28.refs_6_ = f32[4,1,1024,4096]{3,2,1,0:T(8,128)} custom-call(s32[1]{0:T(128)} %bitcast.32.refs_0_, bf16[1024,128]{1,0:T(8,128)(2,1)S(1)} %get-tuple-element.28.refs_1_, bf16[1024,128]{1,0:T(8,128)(2,1)S(1)} %collective-permute-done.3.refs_2_, bf16[1024,128]{1,0:T(8,128)(2,1)S(1)} %collective-permute-done.7.refs_3_, ...), custom_call_target="tpu_custom_call" | custom-call | flops 4294967296 | bytes 20971520 | tf_op jit(solution)/shard_map/pallas_call | solution.py:41
  119.2 9.1 %shard_map.29.refs_6_ = f32[4,1,1024,4096]{3,2,1,0:T(8,128)} custom-call(s32[1]{0:T(128)} %bitcast.31.refs_0_, bf16[1024,128]{1,0:T(8,128)(2,1)S(1)} %collective-permute-done.refs_1_, bf16[1024,128]{1,0:T(8,128)(2,1)S(1)} %collective-permute-done.4.refs_2_, bf16[1024,128]{1,0:T(8,128)(2,1)S(1)} %collective-permute-done.8.refs_3_, ...), custom_call_target="tpu_custom_call", output_to_operand_aliasing={{}: (6, {})} | custom-call | flops 4294967296 | bytes 20971520 | tf_op jit(solution)/shard_map/pallas_call | solution.py:41
  128.3 9.1 %shard_map.30.refs_6_ = f32[4,1,1024,4096]{3,2,1,0:T(8,128)} custom-call(s32[1]{0:T(128)} %bitcast.30.refs_0_, bf16[1024,128]{1,0:T(8,128)(2,1)S(1)} %collective-permute-done.1.refs_1_, bf16[1024,128]{1,0:T(8,128)(2,1)S(1)} %collective-permute-done.5.refs_2_, bf16[1024,128]{1,0:T(8,128)(2,1)S(1)} %collective-permute-done.9.refs_3_, ...), custom_call_target="tpu_custom_call", output_to_operand_aliasing={{}: (6, {})} | custom-call | flops 4294967296 | bytes 20971520 | tf_op jit(solution)/shard_map/pallas_call | solution.py:41
  137.5 9.2 %shard_map.31 = f32[4,1,1024,4096]{3,2,1,0:T(8,128)} custom-call(s32[1]{0:T(128)} %bitcast.refs_0_, bf16[1024,128]{1,0:T(8,128)(2,1)S(1)} %collective-permute-done.2.refs_1_, bf16[1024,128]{1,0:T(8,128)(2,1)S(1)} %collective-permute-done.6.refs_2_, bf16[1024,128]{1,0:T(8,128)(2,1)S(1)} %collective-permute-done.10.refs_3_, ...), custom_call_target="tpu_custom_call", output_to_operand_aliasing={{}: (6, {})} | custom-call | flops 4294967296 | bytes 20971520 | tf_op jit(solution)/shard_map/pallas_call | solution.py:41
  (33 shorter events, 3.7 us)
Async XLA Ops:
  1.9 3.2 %collective-permute-start.3 = (bf16[1024,128]{1,0:T(8,128)(2,1)S(1)}, bf16[1024,128]{1,0:T(8,128)(2,1)S(1)}, u32[]{:S(2)}, u32[]{:S(2)}) collective-permute-start(bf16[1024,128]{1,0:T(8,128)(2,1)S(1)} %get-tuple-element.27), channel_id=1, source_target_pairs={{0,1},{1,0},{2,3},{3,2},{4,5},{5,4},{6,7},{7,6},{8,9},{9,8},{10,11... | collective-permute-start | bytes 786440 | tf_op jit(solution)/shard_map/ppermute | solution.py:13
  2.4 9.7 %collective-permute-start.7 = (bf16[1024,128]{1,0:T(8,128)(2,1)S(1)}, bf16[1024,128]{1,0:T(8,128)(2,1)S(1)}, u32[]{:S(2)}, u32[]{:S(2)}) collective-permute-start(bf16[1024,128]{1,0:T(8,128)(2,1)S(1)} %get-tuple-element.26), channel_id=1, source_target_pairs={{0,2},{1,3},{2,0},{3,1},{4,6},{5,7},{6,4},{7,5},{8,10},{9,11},{10,... | collective-permute-start | bytes 786440 | tf_op jit(solution)/shard_map/ppermute | solution.py:13
  4.9 12.3 %collective-permute-start.11 = (bf16[1024,128]{1,0:T(8,128)(2,1)S(1)}, bf16[1024,128]{1,0:T(8,128)(2,1)S(1)}, u32[]{:S(2)}, u32[]{:S(2)}) collective-permute-start(bf16[1024,128]{1,0:T(8,128)(2,1)S(1)} %get-tuple-element.25), channel_id=1, source_target_pairs={{0,3},{1,2},{2,1},{3,0},{4,7},{5,6},{6,5},{7,4},{8,11},{9,10},{10,... | collective-permute-start | bytes 786440 | tf_op jit(solution)/shard_map/ppermute | solution.py:13
  17.3 26.9 %copy-start = (bf16[1,4,1024,128]{3,2,1,0:T(8,128)(2,1)}, bf16[1,4,1024,128]{3,2,1,0:T(8,128)(2,1)S(1)}, u32[]{:S(2)}) copy-start(bf16[1,4,1024,128]{3,2,1,0:T(8,128)(2,1)S(1)} %maximum_bitcast_fusion) | copy-start | bytes 3145732
  17.3 25.2 %collective-permute-start.15 = (bf16[1,4,1024,128]{3,2,1,0:T(8,128)(2,1)S(1)}, bf16[1,4,1024,128]{3,2,1,0:T(8,128)(2,1)S(1)}, u32[]{:S(2)}, u32[]{:S(2)}) collective-permute-start(bf16[1,4,1024,128]{3,2,1,0:T(8,128)(2,1)S(1)} %maximum_bitcast_fusion), channel_id=1, source_target_pairs={{0,2},{1,3},{2,0},{3,1},{4,6},{5,7},{6,4},{7,5},{8,10},{9,11},{10,... | collective-permute-start | bytes 3145736 | tf_op jit(solution)/shard_map/ppermute | solution.py:13
  42.6 1.7 %copy-start.1 = (bf16[1,4,1024,128]{3,2,1,0:T(8,128)(2,1)}, bf16[1,4,1024,128]{3,2,1,0:T(8,128)(2,1)S(1)}, u32[]{:S(2)}) copy-start(bf16[1,4,1024,128]{3,2,1,0:T(8,128)(2,1)S(1)} %collective-permute-done.15) | copy-start | bytes 3145732
  44.2 53.8 %collective-permute-start.16 = (bf16[2,4,1024,128]{3,2,1,0:T(8,128)(2,1)}, bf16[2,4,1024,128]{3,2,1,0:T(8,128)(2,1)}, u32[]{:S(2)}, u32[]{:S(2)}) collective-permute-start(bf16[2,4,1024,128]{3,2,1,0:T(8,128)(2,1)} %pad_maximum_fusion.1), channel_id=1, source_target_pairs={{0,1},{1,0},{2,3},{3,2},{4,5},{5,4},{6,7},{7,6},{8,9},{9,8},{10,11... | collective-permute-start | bytes 6291464 | tf_op jit(solution)/shard_map/ppermute | solution.py:13
  44.2 11.0 %collective-permute-start = (bf16[1024,128]{1,0:T(8,128)(2,1)S(1)}, bf16[1024,128]{1,0:T(8,128)(2,1)S(1)}, u32[]{:S(2)}, u32[]{:S(2)}) collective-permute-start(bf16[1024,128]{1,0:T(8,128)(2,1)S(1)} %get-tuple-element.28.refs_1_), channel_id=1, source_target_pairs={{0,4},{4,8},{8,12},{12,0},{1,5},{5,9},{9,13},{13,1},{2,6},{6,10},{... | collective-permute-start | bytes 786440 | tf_op jit(solution)/shard_map/ppermute | solution.py:18
  46.1 14.8 %collective-permute-start.12 = (bf16[1024,128]{1,0:T(8,128)(2,1)S(1)}, bf16[1024,128]{1,0:T(8,128)(2,1)S(1)}, u32[]{:S(2)}, u32[]{:S(2)}) collective-permute-start(bf16[1024,128]{1,0:T(8,128)(2,1)S(1)} %collective-permute-done.11.refs_4_), channel_id=1, source_target_pairs={{0,4},{4,8},{8,12},{12,0},{1,5},{5,9},{9,13},{13,1},{2,6},{6,10},{... | collective-permute-start | bytes 786440 | tf_op jit(solution)/shard_map/ppermute | solution.py:18
  47.7 18.8 %collective-permute-start.4 = (bf16[1024,128]{1,0:T(8,128)(2,1)S(1)}, bf16[1024,128]{1,0:T(8,128)(2,1)S(1)}, u32[]{:S(2)}, u32[]{:S(2)}) collective-permute-start(bf16[1024,128]{1,0:T(8,128)(2,1)S(1)} %collective-permute-done.3.refs_2_), channel_id=1, source_target_pairs={{0,4},{4,8},{8,12},{12,0},{1,5},{5,9},{9,13},{13,1},{2,6},{6,10},{... | collective-permute-start | bytes 786440 | tf_op jit(solution)/shard_map/ppermute | solution.py:18
  49.3 22.9 %collective-permute-start.8 = (bf16[1024,128]{1,0:T(8,128)(2,1)S(1)}, bf16[1024,128]{1,0:T(8,128)(2,1)S(1)}, u32[]{:S(2)}, u32[]{:S(2)}) collective-permute-start(bf16[1024,128]{1,0:T(8,128)(2,1)S(1)} %collective-permute-done.7.refs_3_), channel_id=1, source_target_pairs={{0,4},{4,8},{8,12},{12,0},{1,5},{5,9},{9,13},{13,1},{2,6},{6,10},{... | collective-permute-start | bytes 786440 | tf_op jit(solution)/shard_map/ppermute | solution.py:18
  55.3 22.5 %collective-permute-start.1 = (bf16[1024,128]{1,0:T(8,128)(2,1)S(1)}, bf16[1024,128]{1,0:T(8,128)(2,1)S(1)}, u32[]{:S(2)}, u32[]{:S(2)}) collective-permute-start(bf16[1024,128]{1,0:T(8,128)(2,1)S(1)} %collective-permute-done.refs_1_), channel_id=1, source_target_pairs={{0,4},{4,8},{8,12},{12,0},{1,5},{5,9},{9,13},{13,1},{2,6},{6,10},{... | collective-permute-start | bytes 786440 | tf_op jit(solution)/shard_map/ppermute | solution.py:18
  60.9 33.7 %collective-permute-start.13 = (bf16[1024,128]{1,0:T(8,128)(2,1)S(1)}, bf16[1024,128]{1,0:T(8,128)(2,1)S(1)}, u32[]{:S(2)}, u32[]{:S(2)}) collective-permute-start(bf16[1024,128]{1,0:T(8,128)(2,1)S(1)} %collective-permute-done.12.refs_4_), channel_id=1, source_target_pairs={{0,4},{4,8},{8,12},{12,0},{1,5},{5,9},{9,13},{13,1},{2,6},{6,10},{... | collective-permute-start | bytes 786440 | tf_op jit(solution)/shard_map/ppermute | solution.py:18
  66.5 29.6 %collective-permute-start.5 = (bf16[1024,128]{1,0:T(8,128)(2,1)S(1)}, bf16[1024,128]{1,0:T(8,128)(2,1)S(1)}, u32[]{:S(2)}, u32[]{:S(2)}) collective-permute-start(bf16[1024,128]{1,0:T(8,128)(2,1)S(1)} %collective-permute-done.4.refs_2_), channel_id=1, source_target_pairs={{0,4},{4,8},{8,12},{12,0},{1,5},{5,9},{9,13},{13,1},{2,6},{6,10},{... | collective-permute-start | bytes 786440 | tf_op jit(solution)/shard_map/ppermute | solution.py:18
  72.1 22.5 %collective-permute-start.9 = (bf16[1024,128]{1,0:T(8,128)(2,1)S(1)}, bf16[1024,128]{1,0:T(8,128)(2,1)S(1)}, u32[]{:S(2)}, u32[]{:S(2)}) collective-permute-start(bf16[1024,128]{1,0:T(8,128)(2,1)S(1)} %collective-permute-done.8.refs_3_), channel_id=1, source_target_pairs={{0,4},{4,8},{8,12},{12,0},{1,5},{5,9},{9,13},{13,1},{2,6},{6,10},{... | collective-permute-start | bytes 786440 | tf_op jit(solution)/shard_map/ppermute | solution.py:18
  72.2 25.5 %copy-start.2 = (bf16[1,4,1024,128]{3,2,1,0:T(8,128)(2,1)S(1)}, bf16[1,4,1024,128]{3,2,1,0:T(8,128)(2,1)}, u32[]{:S(2)}) copy-start(bf16[1,4,1024,128]{3,2,1,0:T(8,128)(2,1)} %copy-done.1) | copy-start | bytes 3145732
  77.8 59.7 %collective-permute-start.2 = (bf16[1024,128]{1,0:T(8,128)(2,1)S(1)}, bf16[1024,128]{1,0:T(8,128)(2,1)S(1)}, u32[]{:S(2)}, u32[]{:S(2)}) collective-permute-start(bf16[1024,128]{1,0:T(8,128)(2,1)S(1)} %collective-permute-done.1.refs_1_), channel_id=1, source_target_pairs={{0,4},{4,8},{8,12},{12,0},{1,5},{5,9},{9,13},{13,1},{2,6},{6,10},{... | collective-permute-start | bytes 786440 | tf_op jit(solution)/shard_map/ppermute | solution.py:18
  94.6 42.9 %collective-permute-start.10 = (bf16[1024,128]{1,0:T(8,128)(2,1)S(1)}, bf16[1024,128]{1,0:T(8,128)(2,1)S(1)}, u32[]{:S(2)}, u32[]{:S(2)}) collective-permute-start(bf16[1024,128]{1,0:T(8,128)(2,1)S(1)} %collective-permute-done.9.refs_3_), channel_id=1, source_target_pairs={{0,4},{4,8},{8,12},{12,0},{1,5},{5,9},{9,13},{13,1},{2,6},{6,10},{... | collective-permute-start | bytes 786440 | tf_op jit(solution)/shard_map/ppermute | solution.py:18
  94.6 42.9 %collective-permute-start.14 = (bf16[1024,128]{1,0:T(8,128)(2,1)S(1)}, bf16[1024,128]{1,0:T(8,128)(2,1)S(1)}, u32[]{:S(2)}, u32[]{:S(2)}) collective-permute-start(bf16[1024,128]{1,0:T(8,128)(2,1)S(1)} %collective-permute-done.13.refs_4_), channel_id=1, source_target_pairs={{0,4},{4,8},{8,12},{12,0},{1,5},{5,9},{9,13},{13,1},{2,6},{6,10},{... | collective-permute-start | bytes 786440 | tf_op jit(solution)/shard_map/ppermute | solution.py:18
  96.1 41.4 %collective-permute-start.6 = (bf16[1024,128]{1,0:T(8,128)(2,1)S(1)}, bf16[1024,128]{1,0:T(8,128)(2,1)S(1)}, u32[]{:S(2)}, u32[]{:S(2)}) collective-permute-start(bf16[1024,128]{1,0:T(8,128)(2,1)S(1)} %collective-permute-done.5.refs_2_), channel_id=1, source_target_pairs={{0,4},{4,8},{8,12},{12,0},{1,5},{5,9},{9,13},{13,1},{2,6},{6,10},{... | collective-permute-start | bytes 786440 | tf_op jit(solution)/shard_map/ppermute | solution.py:18

commit v2 on v1

v2 whole, which is shorter than its diff:
```python
import jax
import jax.numpy as jnp
from jax import lax
from jax.experimental import pallas as pl
from jax.experimental.pallas import tpu as pltpu
from jax.sharding import PartitionSpec as P

LAGS = 64
VMEM = 48 * 2**20
ANY = pl.BlockSpec(memory_space=pl.ANY)


def pass_on(value, axis):
    count = lax.axis_size(axis)
    return lax.ppermute(value, axis, [(source, (source + 1) % count) for source in range(count)])


def beside(part):
    return jnp.concatenate([part[m] for m in range(part.shape[0])], axis=1)


def exchange(scaled, steps):
    slab_count, piece_rows, slab_len = scaled.shape
    tile_count = lax.axis_size("tile")

    def kernel(scaled_ref, pieces, *refs):
        arrived = refs[:steps]
        own_sem, slab_send, slab_recv, piece_send, piece_recv, ring_send, ring_recv = refs[steps:]
        own = lax.axis_index("tm")
        tile = lax.axis_index("tile")
        right = lax.rem(tile + 1, tile_count)
        left = lax.rem(tile + tile_count - 1, tile_count)

        def remote(source, target, send, recv, device):
            return pltpu.make_async_remote_copy(
                src_ref=source,
                dst_ref=target,
                send_sem=send,
                recv_sem=recv,
                device_id=device,
                device_id_type=pl.DeviceIdType.MESH,
            )

        barrier = pltpu.get_barrier_semaphore()
        others = [{"tm": own ^ m} for m in range(1, slab_count)] + [{"tile": right}, {"tile": left}]
        for other in others:
            pl.semaphore_signal(
                barrier, inc=1, device_id=other, device_id_type=pl.DeviceIdType.MESH
            )
        pl.semaphore_wait(barrier, len(others))

        slabs = {
            m: remote(
                scaled_ref.at[own ^ m],
                pieces.at[0, m],
                slab_send.at[m],
                slab_recv.at[m],
                {"tm": own ^ m},
            )
            for m in range(1, slab_count)
        }

        def ring(step, m):
            if step:
                source = arrived[step - 1].at[m]
            else:
                source = pieces.at[0, m] if m else scaled_ref.at[own]
            return remote(
                source,
                arrived[step].at[m],
                ring_send.at[step, m],
                ring_recv.at[step, m],
                {"tile": right},
            )

        rings = {(step, m): ring(step, m) for step in range(steps) for m in range(slab_count)}
        local = pltpu.make_async_copy(scaled_ref.at[own], pieces.at[0, 0], own_sem)
        for m in reversed(range(1, slab_count)):
            slabs[m].start()
        rings[0, 0].start()
        local.start()
        for m in range(1, slab_count):
            slabs[m].wait_recv()
            rings[0, m].start()
        local.wait()

        held, sent = [0], []
        mask = slab_count // 2
        first = True
        while mask:
            moves = [
                remote(
                    pieces.at[q],
                    pieces.at[q ^ mask],
                    piece_send.at[q ^ mask],
                    piece_recv.at[q ^ mask],
                    {"tm": own ^ mask},
                )
                for q in held
            ]
            for move in moves:
                move.start()
            if first:
                first = False
                for step in range(1, steps):
                    for m in range(slab_count):
                        rings[step - 1, m].wait_recv()
                        rings[step, m].start()
            for move in moves:
                move.wait_recv()
            sent += moves
            held = held + [q ^ mask for q in held]
            mask //= 2
        for m in range(slab_count):
            rings[steps - 1, m].wait_recv()
        for move in [*slabs.values(), *rings.values(), *sent]:
            move.wait_send()

    piece = jax.ShapeDtypeStruct((slab_count, piece_rows, slab_len), jnp.bfloat16)
    everything = jax.ShapeDtypeStruct((slab_count, *piece.shape), jnp.bfloat16)
    dma = pltpu.SemaphoreType.DMA
    return pl.pallas_call(
        kernel,
        out_shape=[everything] + [piece] * steps,
        in_specs=[ANY],
        out_specs=[ANY] * (1 + steps),
        scratch_shapes=[dma(())]
        + [dma((slab_count,))] * 4
        + [dma((steps, slab_count))] * 2,
        compiler_params=pltpu.CompilerParams(collective_id=0, has_side_effects=True),
    )(scaled)


def weigh(pieces, slab_index):
    piece_count, slab_count, piece_rows, slab_len = pieces.shape
    period_count = slab_count * slab_len
    scale = 1.0 / ((LAGS + 1) * period_count)

    def band(own, partner):
        row = lax.broadcasted_iota(jnp.int32, (slab_len, slab_len), 0)
        column = lax.broadcasted_iota(jnp.int32, (slab_len, slab_len), 1)
        distance = row - column
        rows = []
        for u in range(slab_count):
            blocks = []
            for v in range(slab_count):
                apart = ((own ^ u) - (partner ^ v)) * slab_len
                weight = jnp.maximum(0, LAGS + 1 - jnp.abs(distance + apart))
                blocks.append(weight.astype(jnp.float32).astype(jnp.bfloat16))
            rows.append(jnp.concatenate(blocks, axis=1))
        return jnp.concatenate(rows, axis=0)

    def kernel(index_ref, pieces_ref, out_ref):
        own = index_ref[0]
        for q in range(piece_count):
            partner = own ^ q
            product = lax.dot_general(
                band(own, partner),
                beside(pieces_ref[q]),
                (((1,), (1,)), ((), ())),
                preferred_element_type=jnp.float32,
            )
            out_ref[partner] = (product * scale).astype(jnp.bfloat16)

    return pl.pallas_call(
        kernel,
        out_shape=jax.ShapeDtypeStruct((piece_count, period_count, piece_rows), jnp.bfloat16),
        in_specs=[pl.BlockSpec(memory_space=pltpu.SMEM)]
        + [pl.BlockSpec(memory_space=pltpu.VMEM)],
        out_specs=pl.BlockSpec(memory_space=pltpu.VMEM),
        compiler_params=pltpu.CompilerParams(vmem_limit_bytes=VMEM),
        cost_estimate=pl.CostEstimate(
            flops=piece_count * piece_rows * period_count,
            bytes_accessed=piece_rows * period_count,
            transcendentals=0,
        ),
    )(slab_index.reshape(1), pieces)


def write_block(block, piece, weighted, whole, block_count, width=1024):
    slab_count, piece_rows, slab_len = piece.shape[1:]
    chunk_count, period_count, chunk_columns = weighted.shape
    column_step = min(chunk_columns, width)
    split = chunk_columns // column_step

    def kernel(block_ref, piece_ref, weighted_ref, *refs):
        refs[-1][0, 0] = jnp.dot(
            beside(piece_ref[0]), weighted_ref[0], preferred_element_type=jnp.float32
        )

    in_specs = [
        pl.BlockSpec((1, slab_count, piece_rows, slab_len), lambda c, b: (0, 0, 0, 0)),
        pl.BlockSpec(
            (1, period_count, column_step),
            lambda c, b: (lax.div(c, split), 0, lax.rem(c, split)),
        ),
    ]
    operands = [block, piece, weighted]
    aliases = {}
    if whole is not None:
        aliases = {len(operands): 0}
        operands.append(whole)
        in_specs.append(ANY)
    return pl.pallas_call(
        kernel,
        out_shape=jax.ShapeDtypeStruct(
            (block_count, 1, piece_rows, chunk_count * chunk_columns), jnp.float32
        ),
        grid_spec=pltpu.PrefetchScalarGridSpec(
            num_scalar_prefetch=1,
            grid=(chunk_count * split,),
            in_specs=in_specs,
            out_specs=pl.BlockSpec(
                (1, 1, piece_rows, column_step), lambda c, b: (b[0], 0, 0, c)
            ),
        ),
        input_output_aliases=aliases,
        compiler_params=pltpu.CompilerParams(vmem_limit_bytes=VMEM),
        cost_estimate=pl.CostEstimate(
            flops=2 * piece_rows * period_count * chunk_count * chunk_columns,
            bytes_accessed=4 * piece_rows * chunk_count * chunk_columns,
            transcendentals=0,
        ),
    )(*operands)


def local(shocks, volatility):
    scaled = (shocks.astype(jnp.float32) * volatility[:, None]).astype(jnp.bfloat16)
    row_count, slab_len = scaled.shape
    slab_parts = lax.axis_size("tm")
    tile_parts = lax.axis_size("tile")
    slab_index = lax.axis_index("tm")
    tile_index = lax.axis_index("tile")
    piece_rows = row_count // slab_parts

    steps = min(2, tile_parts - 1)
    pieces, *arrived = exchange(scaled.reshape(slab_parts, piece_rows, slab_len), steps)
    while len(arrived) < tile_parts - 1:
        arrived.append(pass_on(arrived[-1], "tile"))
    weighted = weigh(pieces, slab_index)
    if piece_rows % 128:
        weighted = weighted.transpose(1, 0, 2).reshape(1, -1, row_count)
    whole = None
    for step in range(tile_parts):
        block = lax.rem(tile_index - step + tile_parts, tile_parts).reshape(1)
        piece = arrived[step - 1][None] if step else pieces
        whole = write_block(block, piece, weighted, whole, tile_parts)
    return whole


def solution(mesh):
    in_specs = (P(("groups", "tile"), "tm"), P("tile"))
    out_specs = P("groups", "tm", None, "tile")
    return jax.shard_map(local, mesh=mesh, in_specs=in_specs, out_specs=out_specs, check_vma=False)
```

time: 147 us -> 97.8 us (0.67)
  waiting for transfers between devices: 79.6 us -> 0.01 us
  Pallas kernels: 36.7 us -> 92.8 us
  starting transfers between devices: 13 us -> 0.28 us
  matrix products: 9.22 us -> 0 us
  other arithmetic: 4.58 us -> 2.53 us
    pallas_call x4 -> x6, Pallas kernels: 36.7 us -> 92.8 us  [the longest x1 54.4 us: exchange(): pl.pallas_call(kernel, out_shape=[everything] + [piece] * steps, in_specs...]
    ppermute x12 -> x1, waiting for transfers between devices: 43.8 us -> 0.01 us  [pass_on(): lax.ppermute(value, axis, [(source, (source + 1) % count) for source in r...]
    ppermute x5 -> x0, waiting for transfers between devices: 35.8 us -> none  [swap(): lax.ppermute(value, axis, [(source, source ^ mask) for source in range(co...]
    dot_general x1 -> x0, matrix products: 9.22 us -> none  [local(): lax.dot_general(band, series, (((1,), (1,)), ((), ())), preferred_element...]
    ppermute x12 -> x1, starting transfers between devices: 8.22 us -> 0.28 us  [pass_on(): lax.ppermute(value, axis, [(source, (source + 1) % count) for source in r...]
    ppermute x5 -> x0, starting transfers between devices: 4.79 us -> none  [swap(): lax.ppermute(value, axis, [(source, source ^ mask) for source in range(co...]
    squeeze x4 -> x0, local copies, waits for them, and re-layouts: 3.35 us -> none  [the longest x3 3.07 us: local(): pieces[at, m ^ q]]
    unnamed x6 -> x10, local copies, waits for them, and re-layouts: 0.01 us -> 1.98 us
  transfers between devices with their start and end apart: 17 -> 1, of which waited for: 9 -> 0; matrix products, arithmetic and copies ran while one was open for 9% -> 0% of each run, Pallas kernels for 19% -> 31%
where the time goes in v2:
time: 97.8 us; the launch traced here: 97.6 us
  Pallas kernels  92.8 us (95%)
  other arithmetic  2.53 us (3%)
  local copies, waits for them, and re-layouts  1.98 us (2%)
    pallas_call x1, Pallas kernels, exchange(): pl.pallas_call(kernel, out_shape=[everything] + [piece] * steps, in_specs...  54.4 us
    pallas_call x4, Pallas kernels, write_block(): pl.pallas_call(kernel, out_shape=jax.ShapeDtypeStruct((block_count, 1, pi...  33.6 us
    pallas_call x1, Pallas kernels, weigh(): pl.pallas_call(kernel, out_shape=jax.ShapeDtypeStruct((piece_count, perio...  4.72 us
    convert_element_type x1, other arithmetic, local(): (shocks.astype(jnp.float32) * volatility[:, None]).astype(jnp.bfloat16)  2.53 us
    unnamed x10, local copies, waits for them, and re-layouts  1.98 us
  transfers between devices with their start and end apart: 1, of which 0 were waited for; matrix products, arithmetic and copies ran while one was open for 0% of the time, Pallas kernels for 31%

profile of v2, /device:TPU:0, one launch (start us, length us, event | category | flops | bytes accessed | tf_op | source)
XLA Modules:
  0.0 97.6 jit_solution(5302193889351310372)
XLA Ops:
  0.0 2.5 %multiply_convert_fusion = bf16[4096,128]{1,0:T(8,128)(2,1)} fusion(bf16[4096,128]{1,0:T(8,128)(2,1)} %param.2, f32[4096]{0:T(1024)} %param.3), kind=kLoop, calls=%fused_computation | loop fusion | flops 1572864 | bytes 2113536 | tf_op jit(solution)/shard_map/convert_element_type | solution.py:228
  2.5 54.4 %shard_map.28 = (bf16[4,4,1024,128]{3,2,1,0:T(8,128)(2,1)}, bf16[4,1024,128]{2,1,0:T(8,128)(2,1)}, bf16[4,1024,128]{2,1,0:T(8,128)(2,1)}) custom-call(bf16[4,1024,128]{2,1,0:T(8,128)(2,1)} %bitcast.12), custom_call_target="tpu_custom_call" | custom-call | tf_op jit(solution)/shard_map/pallas_call | solution.py:122
  57.0 0.3 collective-permute-start
  57.3 0.0 copy-start.2
  57.3 4.7 %shard_map.29.weighted_ref = bf16[4,512,1024]{2,1,0:T(8,128)(2,1)S(1)} custom-call(s32[1]{0:T(128)} %bitcast.3.index_ref, bf16[4,4,1024,128]{3,2,1,0:T(8,128)(2,1)} %get-tuple-element.9.pieces_ref.piece_ref), custom_call_target="tpu_custom_call" | custom-call | flops 2097152 | bytes 524288 | tf_op jit(solution)/shard_map/pallas_call | solution.py:165
  62.0 0.0 copy-start
  62.0 2.0 %copy-done = bf16[4,512,1024]{2,1,0:T(8,128)(2,1)} copy-done((bf16[4,512,1024]{2,1,0:T(8,128)(2,1)}, bf16[4,512,1024]{2,1,0:T(8,128)(2,1)S(1)}, u32[]{:S(2)}) %copy-start) | copy-done | bytes 4194328
  64.0 0.0 copy-done.2
  64.0 0.0 copy-start.1
  64.0 0.0 copy-start.4
  64.0 9.9 %shard_map.30.refs_0_ = f32[4,1,1024,4096]{3,2,1,0:T(8,128)} custom-call(s32[1]{0:T(128)} %bitcast.8.block_ref, bf16[4,4,1024,128]{3,2,1,0:T(8,128)(2,1)S(1)} %copy-done.2, bf16[4,512,1024]{2,1,0:T(8,128)(2,1)} %copy-done), custom_call_target="tpu_custom_call" | custom-call | flops 4294967296 | bytes 16777216 | tf_op jit(solution)/shard_map/pallas_call | solution.py:204
  73.8 0.0 copy-done.1
  73.8 0.0 copy-done.4
  73.9 0.0 copy-start.3
  73.9 7.9 %shard_map.31.refs_0_ = f32[4,1,1024,4096]{3,2,1,0:T(8,128)} custom-call(s32[1]{0:T(128)} %bitcast.6.block_ref, bf16[1,4,1024,128]{3,2,1,0:T(8,128)(2,1)S(1)} %bitcast.11, bf16[4,512,1024]{2,1,0:T(8,128)(2,1)S(1)} %copy-done.1, f32[4,1,1024,4096]{3,2,1,0:T(8,128)} %shard_map.30.refs_0_), custom_call_target="tpu_custom_call", output_to_operand_aliasing={{}: (3, {})} | custom-call | flops 4294967296 | bytes 16777216 | tf_op jit(solution)/shard_map/pallas_call | solution.py:204
  81.8 0.0 copy-done.3
  81.8 7.9 %shard_map.32.refs_0_ = f32[4,1,1024,4096]{3,2,1,0:T(8,128)} custom-call(s32[1]{0:T(128)} %bitcast.4.block_ref, bf16[1,4,1024,128]{3,2,1,0:T(8,128)(2,1)S(1)} %bitcast.9, bf16[4,512,1024]{2,1,0:T(8,128)(2,1)S(1)} %copy-done.1, f32[4,1,1024,4096]{3,2,1,0:T(8,128)} %shard_map.31.refs_0_), custom_call_target="tpu_custom_call", output_to_operand_aliasing={{}: (3, {})} | custom-call | flops 4294967296 | bytes 16777216 | tf_op jit(solution)/shard_map/pallas_call | solution.py:204
  89.7 0.0 collective-permute-done
  89.7 7.9 %shard_map.33 = f32[4,1,1024,4096]{3,2,1,0:T(8,128)} custom-call(s32[1]{0:T(128)} %bitcast.block_ref, bf16[1,4,1024,128]{3,2,1,0:T(8,128)(2,1)S(1)} %bitcast.10, bf16[4,512,1024]{2,1,0:T(8,128)(2,1)S(1)} %copy-done.1, f32[4,1,1024,4096]{3,2,1,0:T(8,128)} %shard_map.32.refs_0_), custom_call_target="tpu_custom_call", output_to_operand_aliasing={{}: (3, {})} | custom-call | flops 4294967296 | bytes 16777216 | tf_op jit(solution)/shard_map/pallas_call | solution.py:204
Async XLA Ops:
  57.0 32.7 %collective-permute-start = (bf16[4,1024,128]{2,1,0:T(8,128)(2,1)}, bf16[4,1024,128]{2,1,0:T(8,128)(2,1)S(1)}, u32[]{:S(2)}, u32[]{:S(2)}) collective-permute-start(bf16[4,1024,128]{2,1,0:T(8,128)(2,1)} %get-tuple-element.8), channel_id=1, source_target_pairs={{0,4},{4,8},{8,12},{12,0},{1,5},{5,9},{9,13},{13,1},{2,6},{6,10},{... | collective-permute-start | bytes 3145736 | tf_op jit(solution)/shard_map/ppermute | solution.py:15
  57.3 6.7 %copy-start.2 = (bf16[4,4,1024,128]{3,2,1,0:T(8,128)(2,1)S(1)}, bf16[4,4,1024,128]{3,2,1,0:T(8,128)(2,1)}, u32[]{:S(2)}) copy-start(bf16[4,4,1024,128]{3,2,1,0:T(8,128)(2,1)} %get-tuple-element.9.pieces_ref.piece_ref) | copy-start | bytes 12582916
  62.0 2.0 %copy-start = (bf16[4,512,1024]{2,1,0:T(8,128)(2,1)}, bf16[4,512,1024]{2,1,0:T(8,128)(2,1)S(1)}, u32[]{:S(2)}) copy-start(bf16[4,512,1024]{2,1,0:T(8,128)(2,1)S(1)} %shard_map.29.weighted_ref) | copy-start | bytes 12582916
  64.0 9.9 %copy-start.1 = (bf16[4,512,1024]{2,1,0:T(8,128)(2,1)S(1)}, bf16[4,512,1024]{2,1,0:T(8,128)(2,1)}, u32[]{:S(2)}) copy-start(bf16[4,512,1024]{2,1,0:T(8,128)(2,1)} %copy-done) | copy-start | bytes 12582916
  64.0 9.9 %copy-start.4 = (bf16[4,1024,128]{2,1,0:T(8,128)(2,1)S(1)}, bf16[4,1024,128]{2,1,0:T(8,128)(2,1)}, u32[]{:S(2)}) copy-start(bf16[4,1024,128]{2,1,0:T(8,128)(2,1)} %get-tuple-element.10) | copy-start | bytes 3145732
  73.9 8.0 %copy-start.3 = (bf16[4,1024,128]{2,1,0:T(8,128)(2,1)S(1)}, bf16[4,1024,128]{2,1,0:T(8,128)(2,1)}, u32[]{:S(2)}) copy-start(bf16[4,1024,128]{2,1,0:T(8,128)(2,1)} %get-tuple-element.8) | copy-start | bytes 3145732

commit v3 on v2

--- a/solution.py
+++ b/solution.py
@@ -22,6 +22,7 @@
 def exchange(scaled, steps):
     slab_count, piece_rows, slab_len = scaled.shape
     tile_count = lax.axis_size("tile")
+    counts = [slab_count] * (steps - 1) + [slab_count - 1]
 
     def kernel(scaled_ref, pieces, *refs):
         arrived = refs[:steps]
@@ -73,7 +74,7 @@
                 {"tile": right},
             )
 
-        rings = {(step, m): ring(step, m) for step in range(steps) for m in range(slab_count)}
+        rings = {(step, m): ring(step, m) for step in range(steps) for m in range(counts[step])}
         local = pltpu.make_async_copy(scaled_ref.at[own], pieces.at[0, 0], own_sem)
         for m in reversed(range(1, slab_count)):
             slabs[m].start()
@@ -103,7 +104,7 @@
             if first:
                 first = False
                 for step in range(1, steps):
-                    for m in range(slab_count):
+                    for m in range(counts[step]):
                         rings[step - 1, m].wait_recv()
                         rings[step, m].start()
             for move in moves:
@@ -111,17 +112,20 @@
             sent += moves
             held = held + [q ^ mask for q in held]
             mask //= 2
-        for m in range(slab_count):
+        for m in range(counts[-2] - 1, counts[-2]):
+            rings[steps - 2, m].wait_recv()
+        for m in range(counts[-1]):
             rings[steps - 1, m].wait_recv()
         for move in [*slabs.values(), *rings.values(), *sent]:
             move.wait_send()
 
     piece = jax.ShapeDtypeStruct((slab_count, piece_rows, slab_len), jnp.bfloat16)
+    part = jax.ShapeDtypeStruct((slab_count - 1, piece_rows, slab_len), jnp.bfloat16)
     everything = jax.ShapeDtypeStruct((slab_count, *piece.shape), jnp.bfloat16)
     dma = pltpu.SemaphoreType.DMA
     return pl.pallas_call(
         kernel,
-        out_shape=[everything] + [piece] * steps,
+        out_shape=[everything] + [piece] * (steps - 1) + [part],
         in_specs=[ANY],
         out_specs=[ANY] * (1 + steps),
         scratch_shapes=[dma(())]
@@ -177,25 +181,27 @@
     )(slab_index.reshape(1), pieces)
 
 
-def write_block(block, piece, weighted, whole, block_count, width=1024):
-    slab_count, piece_rows, slab_len = piece.shape[1:]
+def write_block(block, parts, weighted, whole, block_count, width=1024):
+    piece_rows = parts[0].shape[2]
     chunk_count, period_count, chunk_columns = weighted.shape
     column_step = min(chunk_columns, width)
     split = chunk_columns // column_step
 
-    def kernel(block_ref, piece_ref, weighted_ref, *refs):
+    def kernel(block_ref, *refs):
+        left = [beside(ref[0]) for ref in refs[: len(parts)]]
+        left = jnp.concatenate(left, axis=1) if len(left) > 1 else left[0]
         refs[-1][0, 0] = jnp.dot(
-            beside(piece_ref[0]), weighted_ref[0], preferred_element_type=jnp.float32
+            left, refs[len(parts)][0], preferred_element_type=jnp.float32
         )
 
     in_specs = [
-        pl.BlockSpec((1, slab_count, piece_rows, slab_len), lambda c, b: (0, 0, 0, 0)),
+        *[pl.BlockSpec((1, *part.shape[1:]), lambda c, b: (0, 0, 0, 0)) for part in parts],
         pl.BlockSpec(
             (1, period_count, column_step),
             lambda c, b: (lax.div(c, split), 0, lax.rem(c, split)),
         ),
     ]
-    operands = [block, piece, weighted]
+    operands = [block, *parts, weighted]
     aliases = {}
     if whole is not None:
         aliases = {len(operands): 0}
@@ -233,18 +239,17 @@
     tile_index = lax.axis_index("tile")
     piece_rows = row_count // slab_parts
 
-    steps = min(2, tile_parts - 1)
-    pieces, *arrived = exchange(scaled.reshape(slab_parts, piece_rows, slab_len), steps)
-    while len(arrived) < tile_parts - 1:
-        arrived.append(pass_on(arrived[-1], "tile"))
+    pieces, near, most = exchange(scaled.reshape(slab_parts, piece_rows, slab_len), 2)
+    arrived = [[pieces], [near[None]], [most[None], pass_on(near[-1:], "tile")[None]]]
+    while len(arrived) < tile_parts:
+        arrived.append([pass_on(part, "tile") for part in arrived[-1]])
     weighted = weigh(pieces, slab_index)
     if piece_rows % 128:
         weighted = weighted.transpose(1, 0, 2).reshape(1, -1, row_count)
     whole = None
     for step in range(tile_parts):
         block = lax.rem(tile_index - step + tile_parts, tile_parts).reshape(1)
-        piece = arrived[step - 1][None] if step else pieces
-        whole = write_block(block, piece, weighted, whole, tile_parts)
+        whole = write_block(block, arrived[step], weighted, whole, tile_parts)
     return whole
 
 

time: 97.8 us -> 95 us (0.971)
  Pallas kernels: 92.8 us -> 87.2 us
  starting transfers between devices: 0.28 us -> 1.4 us
  local copies, waits for them, and re-layouts: 1.98 us -> 2.96 us
    pallas_call x1, Pallas kernels: 54.4 us -> 48.8 us  [exchange(): pl.pallas_call(kernel, out_shape=[everything] + [piece] * (steps - 1) + [...]
    ppermute x1 -> x3, starting transfers between devices: 0.28 us -> 1.4 us  [pass_on(): lax.ppermute(value, axis, [(source, (source + 1) % count) for source in r...]
  transfers between devices with their start and end apart: 1 -> 3, of which waited for: 0 -> 1; matrix products, arithmetic and copies ran while one was open for 0% -> 0% of each run, Pallas kernels for 31% -> 32%
where the time goes in v3:
time: 95 us; the launch traced here: 94.2 us
  Pallas kernels  87.2 us (92%)
  local copies, waits for them, and re-layouts  2.96 us (3%)
  other arithmetic  2.53 us (3%)
  starting transfers between devices  1.4 us (1%)
    pallas_call x1, Pallas kernels, exchange(): pl.pallas_call(kernel, out_shape=[everything] + [piece] * (steps - 1) + [...  48.8 us
    pallas_call x4, Pallas kernels, write_block(): pl.pallas_call(kernel, out_shape=jax.ShapeDtypeStruct((block_count, 1, pi...  33.6 us
    pallas_call x1, Pallas kernels, weigh(): pl.pallas_call(kernel, out_shape=jax.ShapeDtypeStruct((piece_count, perio...  4.72 us
    convert_element_type x1, other arithmetic, local(): (shocks.astype(jnp.float32) * volatility[:, None]).astype(jnp.bfloat16)  2.53 us
    unnamed x10, local copies, waits for them, and re-layouts  1.99 us
  transfers between devices with their start and end apart: 3, of which 1 were waited for; matrix products, arithmetic and copies ran while one was open for 0% of the time, Pallas kernels for 32%

profile of v3, /device:TPU:0, one launch (start us, length us, event | category | flops | bytes accessed | tf_op | source)
XLA Modules:
  0.0 94.2 jit_solution(12191567931335097590)
XLA Ops:
  0.0 2.5 %multiply_convert_fusion = bf16[4096,128]{1,0:T(8,128)(2,1)} fusion(bf16[4096,128]{1,0:T(8,128)(2,1)} %param.2, f32[4096]{0:T(1024)} %param.3), kind=kLoop, calls=%fused_computation | loop fusion | flops 1572864 | bytes 2113536 | tf_op jit(solution)/shard_map/convert_element_type | solution.py:234
  2.5 48.8 %shard_map.28 = (bf16[4,4,1024,128]{3,2,1,0:T(8,128)(2,1)}, bf16[4,1024,128]{2,1,0:T(8,128)(2,1)}, bf16[3,1024,128]{2,1,0:T(8,128)(2,1)}) custom-call(bf16[4,1024,128]{2,1,0:T(8,128)(2,1)} %bitcast.14), custom_call_target="tpu_custom_call" | custom-call | tf_op jit(solution)/shard_map/pallas_call | solution.py:126
  51.4 1.0 %slice.3 = bf16[1,1024,128]{2,1,0:T(8,128)(2,1)S(1)} slice(bf16[4,1024,128]{2,1,0:T(8,128)(2,1)} %get-tuple-element.9), slice={[3:4], [0:1024], [0:128]} | slice | bytes 524288 | tf_op jit(solution)/shard_map/slice | solution.py:243
  52.3 0.3 collective-permute-start.1
  52.6 0.1 collective-permute-start
  52.7 0.0 copy-start.2
  52.7 4.7 %shard_map.29.refs_1_.refs_2_ = bf16[4,512,1024]{2,1,0:T(8,128)(2,1)S(1)} custom-call(s32[1]{0:T(128)} %bitcast.4.index_ref, bf16[4,4,1024,128]{3,2,1,0:T(8,128)(2,1)} %get-tuple-element.10.pieces_ref.refs_0_), custom_call_target="tpu_custom_call" | custom-call | flops 2097152 | bytes 524288 | tf_op jit(solution)/shard_map/pallas_call | solution.py:169
  57.4 0.0 copy-start
  57.4 2.0 %copy-done = bf16[4,512,1024]{2,1,0:T(8,128)(2,1)} copy-done((bf16[4,512,1024]{2,1,0:T(8,128)(2,1)}, bf16[4,512,1024]{2,1,0:T(8,128)(2,1)S(1)}, u32[]{:S(2)}) %copy-start) | copy-done | bytes 4194328
  59.4 0.0 copy-done.2
  59.4 0.0 copy-start.1
  59.4 0.0 copy-start.3
  59.4 9.9 %shard_map.30.refs_2_ = f32[4,1,1024,4096]{3,2,1,0:T(8,128)} custom-call(s32[1]{0:T(128)} %bitcast.8.block_ref, bf16[4,4,1024,128]{3,2,1,0:T(8,128)(2,1)S(1)} %copy-done.2, bf16[4,512,1024]{2,1,0:T(8,128)(2,1)} %copy-done), custom_call_target="tpu_custom_call" | custom-call | flops 4294967296 | bytes 16777216 | tf_op jit(solution)/shard_map/pallas_call | solution.py:210
  69.3 0.0 copy-done.1
  69.3 0.0 copy-done.3
  69.3 0.0 copy-start.4
  69.3 7.9 %shard_map.31.refs_3_ = f32[4,1,1024,4096]{3,2,1,0:T(8,128)} custom-call(s32[1]{0:T(128)} %bitcast.6.block_ref, bf16[1,4,1024,128]{3,2,1,0:T(8,128)(2,1)S(1)} %bitcast.9, bf16[4,512,1024]{2,1,0:T(8,128)(2,1)S(1)} %copy-done.1, f32[4,1,1024,4096]{3,2,1,0:T(8,128)} %shard_map.30.refs_2_), custom_call_target="tpu_custom_call", output_to_operand_aliasing={{}: (3, {})} | custom-call | flops 4294967296 | bytes 16777216 | tf_op jit(solution)/shard_map/pallas_call | solution.py:210
  77.2 0.0 collective-permute-done.1
  77.2 1.1 %collective-permute-start.2 = (bf16[1,1,1024,128]{3,2,1,0:T(8,128)(2,1)S(1)}, bf16[1,1,1024,128]{3,2,1,0:T(8,128)(2,1)S(1)}, u32[]{:S(2)}, u32[]{:S(2)}) collective-permute-start(bf16[1,1,1024,128]{3,2,1,0:T(8,128)(2,1)S(1)} %bitcast.12), channel_id=1, source_target_pairs={{0,4},{4,8},{8,12},{12,0},{1,5},{5,9},{9,13},{13,1},{2,6},{6,10},{... | collective-permute-start | bytes 786440 | tf_op jit(solution)/shard_map/ppermute | solution.py:15
  78.3 0.0 copy-done.4
  78.3 7.9 %shard_map.32.refs_3_ = f32[4,1,1024,4096]{3,2,1,0:T(8,128)} custom-call(s32[1]{0:T(128)} %bitcast.5.block_ref, bf16[1,3,1024,128]{3,2,1,0:T(8,128)(2,1)S(1)} %bitcast.11, bf16[1,1,1024,128]{3,2,1,0:T(8,128)(2,1)S(1)} %bitcast.13, bf16[4,512,1024]{2,1,0:T(8,128)(2,1)S(1)} %copy-done.1, ...), custom_call_target="tpu_custom_call", output_to_operand_aliasing={{}: (4, {})} | custom-call | flops 4294967296 | bytes 16777216 | tf_op jit(solution)/shard_map/pallas_call | solution.py:210
  86.2 0.1 collective-permute-done.2.refs_1_
  86.3 0.0 collective-permute-done.refs_0_
  86.3 7.9 %shard_map.33 = f32[4,1,1024,4096]{3,2,1,0:T(8,128)} custom-call(s32[1]{0:T(128)} %bitcast.block_ref, bf16[1,3,1024,128]{3,2,1,0:T(8,128)(2,1)S(1)} %collective-permute-done.refs_0_, bf16[1,1,1024,128]{3,2,1,0:T(8,128)(2,1)S(1)} %collective-permute-done.2.refs_1_, bf16[4,512,1024]{2,1,0:T(8,128)(2,1)S(1)} %copy-done.1, ...), custom_call_target="tpu_custom_call", output_to_operand_aliasing={{}: (4, {})} | custom-call | flops 4294967296 | bytes 16777216 | tf_op jit(solution)/shard_map/pallas_call | solution.py:210
Async XLA Ops:
  52.3 24.9 %collective-permute-start.1 = (bf16[1,1024,128]{2,1,0:T(8,128)(2,1)S(1)}, bf16[1,1024,128]{2,1,0:T(8,128)(2,1)S(1)}, u32[]{:S(2)}, u32[]{:S(2)}) collective-permute-start(bf16[1,1024,128]{2,1,0:T(8,128)(2,1)S(1)} %slice.3), channel_id=1, source_target_pairs={{0,4},{4,8},{8,12},{12,0},{1,5},{5,9},{9,13},{13,1},{2,6},{6,10},{... | collective-permute-start | bytes 786440 | tf_op jit(solution)/shard_map/ppermute | solution.py:15
  52.6 33.7 %collective-permute-start = (bf16[1,3,1024,128]{3,2,1,0:T(8,128)(2,1)}, bf16[1,3,1024,128]{3,2,1,0:T(8,128)(2,1)S(1)}, u32[]{:S(2)}, u32[]{:S(2)}) collective-permute-start(bf16[1,3,1024,128]{3,2,1,0:T(8,128)(2,1)} %bitcast.10), channel_id=1, source_target_pairs={{0,4},{4,8},{8,12},{12,0},{1,5},{5,9},{9,13},{13,1},{2,6},{6,10},{... | collective-permute-start | bytes 2359304 | tf_op jit(solution)/shard_map/ppermute | solution.py:15
  52.7 6.7 %copy-start.2 = (bf16[4,4,1024,128]{3,2,1,0:T(8,128)(2,1)S(1)}, bf16[4,4,1024,128]{3,2,1,0:T(8,128)(2,1)}, u32[]{:S(2)}) copy-start(bf16[4,4,1024,128]{3,2,1,0:T(8,128)(2,1)} %get-tuple-element.10.pieces_ref.refs_0_) | copy-start | bytes 12582916
  57.4 2.0 %copy-start = (bf16[4,512,1024]{2,1,0:T(8,128)(2,1)}, bf16[4,512,1024]{2,1,0:T(8,128)(2,1)S(1)}, u32[]{:S(2)}) copy-start(bf16[4,512,1024]{2,1,0:T(8,128)(2,1)S(1)} %shard_map.29.refs_1_.refs_2_) | copy-start | bytes 12582916
  59.4 9.9 %copy-start.1 = (bf16[4,512,1024]{2,1,0:T(8,128)(2,1)S(1)}, bf16[4,512,1024]{2,1,0:T(8,128)(2,1)}, u32[]{:S(2)}) copy-start(bf16[4,512,1024]{2,1,0:T(8,128)(2,1)} %copy-done) | copy-start | bytes 12582916
  59.4 9.9 %copy-start.3 = (bf16[4,1024,128]{2,1,0:T(8,128)(2,1)S(1)}, bf16[4,1024,128]{2,1,0:T(8,128)(2,1)}, u32[]{:S(2)}) copy-start(bf16[4,1024,128]{2,1,0:T(8,128)(2,1)} %get-tuple-element.9) | copy-start | bytes 3145732
  69.3 9.0 %copy-start.4 = (bf16[3,1024,128]{2,1,0:T(8,128)(2,1)S(1)}, bf16[3,1024,128]{2,1,0:T(8,128)(2,1)}, u32[]{:S(2)}) copy-start(bf16[3,1024,128]{2,1,0:T(8,128)(2,1)} %get-tuple-element.8) | copy-start | bytes 2359300
  77.2 9.0 %collective-permute-start.2 = (bf16[1,1,1024,128]{3,2,1,0:T(8,128)(2,1)S(1)}, bf16[1,1,1024,128]{3,2,1,0:T(8,128)(2,1)S(1)}, u32[]{:S(2)}, u32[]{:S(2)}) collective-permute-start(bf16[1,1,1024,128]{3,2,1,0:T(8,128)(2,1)S(1)} %bitcast.12), channel_id=1, source_target_pairs={{0,4},{4,8},{8,12},{12,0},{1,5},{5,9},{9,13},{13,1},{2,6},{6,10},{... | collective-permute-start | bytes 786440 | tf_op jit(solution)/shard_map/ppermute | solution.py:15
